TPU v7x, 32 devices: a whole 2x2x4 slice. The times are simulated.
32 devices in a mesh: leaf: 2 (over core), front: 16 (over z, y, x).
Axes of the slice: x: 2, y: 2, z: 4, core: 2. Of those that a mesh axis runs over, the one named last changes fastest.
Arguments:
- front_block: float32 [8192, 8192], P('leaf', 'front'), as said below
- child_update: float32 [2, 6144, 8192], P('leaf', None, 'front'), as said below
- child_map: int32 [2, 48], P('leaf'), may hold values from 0 to 63, as said below
Outputs:
- factored: float32 [8192, 8192], P('leaf', 'front')
Inputs may be any that keep to these rules, and one draw needn't show every extreme that they name: `child_map`: each row is strictly increasing, holds 48 distinct blocks, and always names block 0 and block 63. `front_block`: Symmetric; the assembled front is positive definite. `child_update`: each child's update is symmetric and positive semidefinite in the child's order; columns of parent blocks that the child's map does not name are zero.
All inputs are finite; a program needn't handle non-finite values.
Results may differ from a plain program's by a relative error of at most 0.000088.
Values sent between devices are 32-bit elements; how exact they have to be, the bound alone decides.
No kernel may reach another device: no remote copies, remote signals or barrier semaphores. Data moves between devices by JAX's collectives and lax.ppermute only.
A program may use at most 128 MiB of HBM per device.

v0:
```python
import jax
import jax.numpy as jnp
from jax import lax
from jax.sharding import PartitionSpec as P

BLK = 128
P_SIZE = 8192
S = 512


def spread(block, axis, holder):
    block = jnp.where(lax.axis_index(axis) == holder, block, jnp.zeros_like(block))
    return lax.psum(block, axis)


def solve_right(factor, rows):
    return lax.linalg.triangular_solve(factor, rows, left_side=False, lower=True, transpose_a=True)


def per_device(front_block, child_update, child_map):
    row_count = front_block.shape[0]
    col_count = front_block.shape[1]
    leaf_count = lax.axis_size("leaf")
    leaf_index = lax.axis_index("leaf")
    front_index = lax.axis_index("front")
    offsets = jnp.arange(BLK, dtype=jnp.int32)
    row_index = (child_map[0][:, None] * BLK + offsets[None, :]).reshape(-1)
    placed_rows = jnp.zeros((P_SIZE, col_count), jnp.float32).at[row_index].set(child_update[0])
    received = lax.all_to_all(
        placed_rows.reshape(leaf_count, row_count, col_count),
        "leaf",
        split_axis=0,
        concat_axis=0,
        tiled=True,
    )
    contribution = jnp.sum(received, axis=0)
    assembled = front_block + contribution
    holder = front_index * col_count < S
    zero_panel = jnp.zeros((row_count, S), jnp.float32)
    placed = lax.dynamic_update_slice_in_dim(
        zero_panel, jnp.where(holder, assembled, 0.0), front_index * col_count, 1
    )
    pivot_panel = lax.psum(placed, "front")
    top_block = pivot_panel[:S]
    diag_block, top_cols = (spread(top_block, "leaf", 0), spread(assembled[:S], "leaf", 0))
    factor = jnp.linalg.cholesky(diag_block)
    col_solved = solve_right(factor, top_cols.T)
    solved = solve_right(factor, pivot_panel)
    row_global = leaf_index * row_count + jnp.arange(row_count, dtype=jnp.int32)
    col_global = front_index * col_count + jnp.arange(col_count, dtype=jnp.int32)
    col_start = jnp.minimum(front_index * col_count, S - col_count)
    left_rows = lax.dynamic_slice_in_dim(solved, col_start, col_count, 1)
    left_top = jnp.pad(
        lax.dynamic_slice_in_dim(factor, col_start, col_count, 1), ((0, row_count - S), (0, 0))
    )
    left_part = jnp.where(row_global[:, None] < S, left_top, left_rows)
    schur_part = assembled - jnp.dot(solved, col_solved.T, precision=lax.Precision.HIGHEST)
    right_top = jnp.pad(col_solved.T, ((0, row_count - S), (0, 0)))
    right_part = jnp.where(row_global[:, None] < S, right_top, schur_part)
    return jnp.where(col_global[None, :] < S, left_part, right_part)


def solution(mesh):
    return jax.shard_map(
        per_device,
        mesh=mesh,
        in_specs=(P("leaf", "front"), P("leaf", None, "front"), P("leaf", None)),
        out_specs=P("leaf", "front"),
        check_vma=False,
    )
```

profile of v0, /device:TPU:0, one launch (start us, length us, event | category | flops | bytes accessed | tf_op | source)
XLA Modules:
  0.0 599.4 jit_solution(14588104439594012609)
XLA Ops:
  7.3 33.9 %scatter_custom_fusion = f32[8192,512]{1,0:T(8,128)} fusion(s32[6144]{0:T(1024)S(1)} %bitcast.68, f32[1,6144,512]{2,1,0:T(8,128)} %param.4, f32[]{:T(128)} %constant.166.clone.1), kind=kCustom, calls=%fused_computation.3 | custom fusion | bytes 29360132 | tf_op jit(solution)/shard_map/scatter | solution.py:28
  41.2 9.7 %all-to-all-start = ((f32[2,4096,512]{2,1,0:T(8,128)}), f32[2,4096,512]{2,1,0:T(8,128)}, u32[]{:S(2)}, u32[]{:S(2)}) async-start(f32[2,4096,512]{2,1,0:T(8,128)} %bitcast.66), calls=%async_computation | async-start | bytes 33554432 | tf_op jit(solution)/shard_map/all_to_all | solution.py:29
  51.0 13.4 %all-to-all-done = f32[2,4096,512]{2,1,0:T(8,128)} async-done(((f32[2,4096,512]{2,1,0:T(8,128)}), f32[2,4096,512]{2,1,0:T(8,128)}, u32[]{:S(2)}, u32[]{:S(2)}) %all-to-all-start) | async-done | bytes 16777248 | tf_op jit(solution)/shard_map/all_to_all | solution.py:29
  64.4 12.1 %reduce_sum.9 = f32[4096,512]{1,0:T(8,128)} reduce(f32[2,4096,512]{2,1,0:T(8,128)} %all-to-all-done, f32[]{:T(128)} %constant.166.clone.1), dimensions={0}, to_apply=%region_1.0 | reduce | flops 2097152 | bytes 25165828 | tf_op jit(solution)/shard_map/reduce_sum | solution.py:36
  76.5 8.9 %copy.21 = f32[4096,512]{0,1:T(8,128)} copy(f32[4096,512]{1,0:T(8,128)} %reduce_sum.9) | data formatting | bytes 16777216 | tf_op jit(solution)/shard_map/reduce_sum | solution.py:36
  85.4 8.9 %copy.20 = f32[4096,512]{0,1:T(8,128)} copy(f32[4096,512]{1,0:T(8,128)} %param.3) | data formatting | bytes 16777216 | tf_op args[0]
  94.3 10.8 %broadcast_select_fusion = (f32[4096,512]{0,1:T(8,128)}, f32[4096,512]{0,1:T(8,128)}) fusion(pred[]{:T(512)S(6)} %lt.42, f32[4096,512]{0,1:T(8,128)} %copy.20, f32[4096,512]{0,1:T(8,128)} %copy.21), kind=kLoop, calls=%fused_computation.20 | loop fusion | flops 4194304 | bytes 33554432 | tf_op jit(solution)/shard_map/jit(_where)/select_n | solution.py:41
  107.8 256.6 %all-reduce.7.cloned.1.call-done = f32[4096,512]{0,1:T(8,128)} async-done(((f32[4096,512]{0,1:T(8,128)}), f32[4096,512]{0,1:T(8,128)}) %all-reduce.7.cloned.1.call-update) | async-done | bytes 8388624 | tf_op jit(solution)/shard_map/psum | solution.py:43
  366.7 20.4 %all-reduce.9.cloned.1.call-done = (f32[512,512]{1,0:T(8,128)}, f32[512,512]{0,1:T(8,128)}) async-done(((f32[512,512]{1,0:T(8,128)}, f32[512,512]{0,1:T(8,128)}), (f32[512,512]{1,0:T(8,128)}, f32[512,512]{0,1:T(8,128)})) %all-reduce.9.cloned.1.call-update) | async-done | bytes 2097168 | tf_op jit(solution)/shard_map/psum | solution.py:13
  390.1 11.7 %cholesky.103 = f32[128,128]{1,0:T(8,128)S(1)} custom-call(f32[128,128]{1,0:T(8,128)S(1)} %cholesky.263), custom_call_target="Cholesky" | custom-call | tf_op jit(solution)/shard_map/jit(cholesky)/cholesky | solution.py:46
  401.9 9.8 %custom-call.32 = f32[1,128,128]{1,2,0:T(8,128)S(1)} custom-call(f32[1,128,128]{2,1,0:T(8,128)S(1)} %get-tuple-element.42), custom_call_target="InvertDiagBlocksLowerTriangular" | custom-call | tf_op jit(solution)/shard_map/jit(cholesky)/cholesky | solution.py:46
  412.3 11.7 %cholesky.215 = f32[128,128]{1,0:T(8,128)S(1)} custom-call(f32[128,128]{1,0:T(8,128)S(1)} %cholesky.267), custom_call_target="Cholesky" | custom-call | tf_op jit(solution)/shard_map/jit(cholesky)/cholesky | solution.py:46
  424.6 10.2 %custom-call.33 = f32[1,128,128]{1,2,0:T(8,128)S(1)} custom-call(f32[1,128,128]{2,1,0:T(8,128)S(1)} %get-tuple-element.40), custom_call_target="InvertDiagBlocksLowerTriangular" | custom-call | tf_op jit(solution)/shard_map/jit(cholesky)/cholesky | solution.py:46
  435.8 11.7 %cholesky.236 = f32[128,128]{1,0:T(8,128)S(1)} custom-call(f32[128,128]{1,0:T(8,128)S(1)} %cholesky.272), custom_call_target="Cholesky" | custom-call | tf_op jit(solution)/shard_map/jit(cholesky)/cholesky | solution.py:46
  447.6 9.8 %custom-call.34 = f32[1,128,128]{1,2,0:T(8,128)S(1)} custom-call(f32[1,128,128]{2,1,0:T(8,128)S(1)} %get-tuple-element.38), custom_call_target="InvertDiagBlocksLowerTriangular" | custom-call | tf_op jit(solution)/shard_map/jit(cholesky)/cholesky | solution.py:46
  458.2 11.9 %cholesky.253 = f32[128,128]{1,0:T(8,128)S(1)} custom-call(f32[128,128]{1,0:T(8,128)S(1)} %convolution_subtract_fusion.7), custom_call_target="Cholesky" | custom-call | tf_op jit(solution)/shard_map/jit(cholesky)/cholesky | solution.py:46
  476.0 8.4 %while.1 = (s32[]{:T(128)}, f32[512,512]{0,1:T(8,128)S(1)}, s32[4,2]{0,1:T(2,128)S(1)}, f32[4,128,128]{2,1,0:T(8,128)S(1)}, s32[]{:T(128)}) while((s32[]{:T(128)}, f32[512,512]{0,1:T(8,128)S(1)}, s32[4,2]{0,1:T(2,128)S(1)}, f32[4,128,128]{2,1,0:T(8,128)S(1)}, s32[]{:T(128)}) %tuple.27), condition=%wide.while_cond, body=%wide.while_body.sunk | while | flops 2 | bytes 393321 | solution.py:17
  484.5 39.3 %custom-call.35 = f32[4,128,128]{1,2,0:T(8,128)S(1)} custom-call(f32[4,128,128]{2,1,0:T(8,128)S(1)} %get-tuple-element.12), custom_call_target="InvertDiagBlocksLowerTriangular" | custom-call | tf_op jit(solution)/shard_map/triangular_solve | solution.py:17
  535.2 3.6 fusion.15
  538.8 3.7 convolution_subtract_fusion.1
  544.4 4.4 convolution_subtract_fusion
  550.9 6.1 %fusion.9 = f32[4096,128]{0,1:T(8,128)S(1)} fusion(f32[4096,128]{0,1:T(8,128)S(1)} %fusion.49, f32[4096,128]{0,1:T(8,128)S(1)} %fusion.47, f32[4096,128]{0,1:T(8,128)S(1)} %fusion.15, f32[4096,512]{0,1:T(8,128)} %all-reduce.7.cloned.1.call-done, f32[512,512]{0,1:T(8,128)} %copy-done), kind=kOutput, calls=%fused_computation.16 | convolution fusion | flops 2419589120 | bytes 10682368 | tf_op jit(solution)/shard_map/triangular_solve | solution.py:17
  561.9 21.3 %select_select_fusion = f32[4096,512]{0,1:T(8,128)} fusion(f32[4096,512]{0,1:T(8,128)} %get-tuple-element.34, f32[512,512]{0,1:T(8,128)} %fusion.25, f32[512,512]{0,1:T(8,128)} %get-tuple-element.32, f32[4096,128]{0,1:T(8,128)} %fusion.51, f32[4096,128]{0,1:T(8,128)S(1)} %fusion.49, f32[4096,128]{0,1:T(8,128)S(1)} %fusion.47, f32[4096,128]{0,1:T(8,128)S(1)} %fusion.15, ...), kind=kOutput, calls=%fused_computation.6 | convolution fusion | flops 12906659840 | bytes 28316160 | tf_op jit(solution)/shard_map/dot_general | solution.py:57
  583.1 8.9 %copy.36 = f32[4096,512]{1,0:T(8,128)} copy(f32[4096,512]{0,1:T(8,128)} %select_select_fusion) | data formatting | bytes 16777216 | tf_op jit(solution)/shard_map/jit(_where)/select_n | solution.py:60
  (89 shorter events, 43.6 us)
Async XLA Ops:
  41.2 23.2 %all-to-all-start = ((f32[2,4096,512]{2,1,0:T(8,128)}), f32[2,4096,512]{2,1,0:T(8,128)}, u32[]{:S(2)}, u32[]{:S(2)}) async-start(f32[2,4096,512]{2,1,0:T(8,128)} %bitcast.66), calls=%async_computation | async-start | bytes 33554432 | tf_op jit(solution)/shard_map/all_to_all | solution.py:29
  50.9 313.4 %all-reduce.7.cloned.1.call-start = ((), (), s32[]{:S(2)}) async-start(), calls=%async_computation.1 | async-start | bytes 16777216 | tf_op jit(solution)/shard_map/psum | solution.py:43
  105.2 281.9 %all-reduce.9.cloned.1.call-start = ((), (), s32[]{:S(2)}) async-start(), calls=%async_computation.2 | async-start | bytes 4194304 | tf_op jit(solution)/shard_map/psum | solution.py:13
  484.4 60.0 %copy-start = (f32[512,512]{0,1:T(8,128)}, f32[512,512]{0,1:T(8,128)S(1)}, u32[]{:S(2)}) copy-start(f32[512,512]{0,1:T(8,128)S(1)} %get-tuple-element.99) | copy-start | bytes 3145732
  550.9 9.5 %copy-start.1 = (f32[512,128]{1,0:T(8,128)S(1)}, f32[512,128]{1,0:T(8,128)}, u32[]{:S(2)}) copy-start(f32[512,128]{1,0:T(8,128)} %convolution_subtract_fusion.4) | copy-start | bytes 786436
  550.9 9.9 %copy-start.2 = (f32[512,128]{1,0:T(8,128)S(1)}, f32[512,128]{1,0:T(8,128)}, u32[]{:S(2)}) copy-start(f32[512,128]{1,0:T(8,128)} %copy.33) | copy-start | bytes 786436
  550.9 9.9 %copy-start.3 = (f32[512,128]{1,0:T(8,128)S(1)}, f32[512,128]{1,0:T(8,128)}, u32[]{:S(2)}) copy-start(f32[512,128]{1,0:T(8,128)} %copy.32) | copy-start | bytes 786436
  550.9 9.9 %copy-start.4 = (f32[512,128]{1,0:T(8,128)S(1)}, f32[512,128]{1,0:T(8,128)}, u32[]{:S(2)}) copy-start(f32[512,128]{1,0:T(8,128)} %copy.31) | copy-start | bytes 786436
  560.8 1.1 copy-start.5
Sparse Core Ops, SparseCore 0:
  105.3 258.9 all-reduce.6
  366.8 20.2 all-reduce.8
where the time goes:
time: 608 us; the launch traced here: 599 us
  waiting for transfers between devices  290 us (48%)
  other arithmetic  150 us (25%)
  local copies, waits for them, and re-layouts  73.8 us (12%)
  matrix products  57.9 us (10%)
  between operations  16.8 us (3%)
  starting transfers between devices  9.98 us (2%)
    psum x1, waiting for transfers between devices, per_device(): pivot_panel = lax.psum(placed, 'front')  257 us
    another operation x14, other arithmetic, per_device(): factor = jnp.linalg.cholesky(diag_block)  79 us
    another operation x3, other arithmetic, solve_right(): lax.linalg.triangular_solve(factor, rows, left_side=False, lower=True, tr...  40.6 us
    another operation x14, matrix products, solve_right(): lax.linalg.triangular_solve(factor, rows, left_side=False, lower=True, tr...  34.3 us
    scatter x1, local copies, waits for them, and re-layouts, per_device(): jnp.zeros((P_SIZE, col_count), jnp.float32).at[row_index]  33.9 us
    dot_general x1, matrix products, per_device(): jnp.dot(solved, col_solved.T, precision=lax.Precision.HIGHEST)  21.3 us
    psum x1, waiting for transfers between devices, spread(): return lax.psum(block, axis)  20.4 us
    all_to_all x1, waiting for transfers between devices, per_device(): lax.all_to_all(placed_rows.reshape(leaf_count, row_count, col_count), 'le...  13.4 us
  transfers between devices with their start and end apart: 3, of which 3 were waited for; matrix products, arithmetic and copies ran while one was open for 0% of the time, Pallas kernels for 0%

commit v1 on v0

v1 whole, which is shorter than its diff:
```python
import functools

import jax
import jax.numpy as jnp
from jax import lax
from jax.experimental import pallas as pl
from jax.experimental.pallas import tpu as pltpu
from jax.sharding import PartitionSpec as P

BLK = 128
S = 512
SUB = 8
ROWS = 512
MIB = 1024 * 1024


def lane_spread(tile, lane):
    return jnp.broadcast_to(tile[:, lane:lane + 1], tile.shape)


def row_spread(tile, row):
    return jnp.broadcast_to(tile[row:row + 1, :], tile.shape)


def eliminate_block(block):
    strips = BLK // SUB
    sub = lax.broadcasted_iota(jnp.int32, (SUB, BLK), 0)
    lane = lax.broadcasted_iota(jnp.int32, (SUB, BLK), 1)
    upper = [block[SUB * s:SUB * s + SUB, :] for s in range(strips)]
    lower = [jnp.where(lane == sub + SUB * s, 1.0, 0.0) for s in range(strips)]
    pivots = []
    for p in range(strips):
        first = SUB * p
        cols = [lane_spread(upper[p], first + j) for j in range(SUB)]
        a, x = upper[p], lower[p]
        recips = []
        pivot = jnp.zeros((SUB, BLK), jnp.float32)
        for j in range(SUB):
            d = row_spread(cols[j], j)
            recip = 1.0 / d
            recips.append(recip)
            pivot = jnp.where(sub == j, d, pivot)
            if j + 1 < SUB:
                m = jnp.where(sub > j, cols[j] * recip, 0.0)
                for k in range(j + 1, SUB):
                    cols[k] = cols[k] - m * row_spread(cols[k], j)
                a = a - m * row_spread(a, j)
                x = x - m * row_spread(x, j)
        upper[p], lower[p] = a, x
        pivots.append(pivot)
        if p + 1 == strips:
            break
        va = [row_spread(a, j) * recips[j] for j in range(SUB)]
        vx = [row_spread(x, j) * recips[j] for j in range(SUB)]
        for j in range(SUB - 2, -1, -1):
            for k in range(j + 1, SUB):
                c = row_spread(cols[k], j) * recips[j]
                va[j] = va[j] - c * va[k]
                vx[j] = vx[j] - c * vx[k]
        for s in range(p + 1, strips):
            b = [lane_spread(upper[s], first + j) for j in range(SUB)]
            upper[s] = upper[s] - (
                ((b[0] * va[0] + b[1] * va[1]) + (b[2] * va[2] + b[3] * va[3]))
                + ((b[4] * va[4] + b[5] * va[5]) + (b[6] * va[6] + b[7] * va[7]))
            )
            lower[s] = lower[s] - (
                ((b[0] * vx[0] + b[1] * vx[1]) + (b[2] * vx[2] + b[3] * vx[3]))
                + ((b[4] * vx[4] + b[5] * vx[5]) + (b[6] * vx[6] + b[7] * vx[7]))
            )
    return (
        jnp.concatenate(upper, axis=0),
        jnp.concatenate(lower, axis=0),
        jnp.concatenate(pivots, axis=0),
    )


def exact_dot(a, b, dims=((1,), (0,))):
    return lax.dot_general(
        a, b, (dims, ((), ())),
        precision=lax.Precision.HIGHEST,
        preferred_element_type=jnp.float32,
    )


def factor_kernel(place, diag_ref, cols_ref, top_ref, mult_ref, u_ref, x_ref):
    cc = cols_ref.shape[1]
    u_ref[...] = diag_ref[...]
    eye = lax.broadcasted_iota(jnp.int32, (S, S), 0) == lax.broadcasted_iota(
        jnp.int32, (S, S), 1)
    x_ref[...] = jnp.where(eye, 1.0, 0.0)

    @pl.loop(0, S // BLK)
    def _(step):
        start = pl.multiple_of(step * BLK, BLK)
        rows = pl.ds(start, BLK)
        block, inverse, pivots = eliminate_block(u_ref[rows, rows])
        scale = lax.rsqrt(pivots)
        scale = scale * (1.5 - 0.5 * pivots * scale * scale)
        r = lax.broadcasted_iota(jnp.int32, (BLK, BLK), 0)
        c = lax.broadcasted_iota(jnp.int32, (BLK, BLK), 1)
        block = jnp.where(c >= r, block * scale, 0.0)
        inverse = inverse * scale
        u = exact_dot(inverse, u_ref[rows, :])
        x = exact_dot(inverse, x_ref[rows, :])
        col = lax.broadcasted_iota(jnp.int32, (BLK, S), 1)
        u = jnp.where(col >= start + BLK, u, 0.0)

        @pl.when(step < S // BLK - 1)
        def _():
            u_ref[...] -= exact_dot(u, u, ((0,), (0,)))
            x_ref[...] -= exact_dot(u, x, ((0,), (0,)))

        u_ref[rows, :] = u
        u_ref[rows, rows] = block
        x_ref[rows, :] = x

    is_pivot = place[0] < S // cc
    start = pl.multiple_of(jnp.minimum(place[0], S // cc - 1) * cc, cc)
    solved = exact_dot(x_ref[...], cols_ref[...])
    top_ref[...] = jnp.where(is_pivot, u_ref[pl.ds(start, cc), :].T, solved)
    unit = lax.broadcasted_iota(jnp.int32, (S, cc), 0) == start + lax.broadcasted_iota(
        jnp.int32, (S, cc), 1)
    right = jnp.where(is_pivot, jnp.where(unit, -1.0, 0.0), solved)
    mult_ref[...] = exact_dot(x_ref[...], right, ((0,), (0,)))


def factor_and_solve(place, diag, cols):
    cc = cols.shape[1]
    vmem = pl.BlockSpec(memory_space=pltpu.VMEM)
    flops = 6 * (2 * S * S * cc * 2 + S * S * S * 2)
    return pl.pallas_call(
        factor_kernel,
        out_shape=[jax.ShapeDtypeStruct((S, cc), jnp.float32)] * 2,
        in_specs=[pl.BlockSpec(memory_space=pltpu.SMEM), vmem, vmem],
        out_specs=[vmem, vmem],
        scratch_shapes=[pltpu.VMEM((S, S), jnp.float32)] * 2,
        compiler_params=pltpu.CompilerParams(vmem_limit_bytes=32 * MIB),
        cost_estimate=pl.CostEstimate(
            flops=flops, bytes_accessed=4 * S * (S + 3 * cc), transcendentals=0),
        name="factor_and_solve",
    )(place, diag, cols)


def assemble_kernel(index, front_ref, own_ref, recv_ref, out_ref):
    step = pl.program_id(0)
    own = jnp.where(index[1, step] > 0, own_ref[...], 0.0)
    recv = jnp.where(index[3, step] > 0, recv_ref[...], 0.0)
    out_ref[...] = front_ref[...] + own + recv


def assemble(index, front, child, recv):
    rows, cc = front.shape
    spec = functools.partial(pl.BlockSpec, (BLK, cc))
    return pl.pallas_call(
        assemble_kernel,
        out_shape=jax.ShapeDtypeStruct((rows, cc), jnp.float32),
        grid_spec=pltpu.PrefetchScalarGridSpec(
            num_scalar_prefetch=1,
            grid=(rows // BLK,),
            in_specs=[
                spec(lambda i, index: (i, 0)),
                spec(lambda i, index: (index[0, i], 0)),
                spec(lambda i, index: (index[2, i], 0)),
            ],
            out_specs=spec(lambda i, index: (i, 0)),
        ),
        cost_estimate=pl.CostEstimate(
            flops=2 * rows * cc, bytes_accessed=16 * rows * cc, transcendentals=0),
        name="assemble",
    )(index, front, child, recv)


def finish_kernel(place, base_ref, panel_ref, mult_ref, top_ref, out_ref):
    cc = out_ref.shape[1]
    is_pivot = place[0] < S // cc
    is_top = jnp.logical_and(place[1] == 0, pl.program_id(0) * ROWS < S)

    @pl.when(is_top)
    def _():
        out_ref[...] = top_ref[...]

    @pl.when(jnp.logical_not(is_top))
    def _():
        product = lax.dot_general(
            panel_ref[...], mult_ref[...], (((1,), (0,)), ((), ())),
            precision=lax.Precision.HIGH,
            preferred_element_type=jnp.float32,
        )
        out_ref[...] = jnp.where(is_pivot, 0.0, base_ref[...]) - product


def finish(place, base, panel, mult, top):
    rows, cc = base.shape
    whole = pl.BlockSpec((S, cc), lambda i, place: (0, 0))
    return pl.pallas_call(
        finish_kernel,
        out_shape=jax.ShapeDtypeStruct((rows, cc), jnp.float32),
        grid_spec=pltpu.PrefetchScalarGridSpec(
            num_scalar_prefetch=1,
            grid=(rows // ROWS,),
            in_specs=[
                pl.BlockSpec((ROWS, cc), lambda i, place: (i, 0)),
                pl.BlockSpec((ROWS, S), lambda i, place: (i, 0)),
                whole,
                whole,
            ],
            out_specs=pl.BlockSpec((ROWS, cc), lambda i, place: (i, 0)),
        ),
        compiler_params=pltpu.CompilerParams(vmem_limit_bytes=32 * MIB),
        cost_estimate=pl.CostEstimate(
            flops=6 * rows * S * cc, bytes_accessed=4 * rows * (2 * cc + S),
            transcendentals=0),
        name="finish",
    )(place, base, panel, mult, top)


def block_places(blocks, first, count, shift, limit):
    parent = first + jnp.arange(count, dtype=jnp.int32)
    reached = jnp.sum((blocks[None, :] <= parent[:, None]).astype(jnp.int32), axis=1)
    there = jnp.sum((blocks[None, :] == parent[:, None]).astype(jnp.int32), axis=1)
    return jnp.clip(reached - 1 - shift, 0, limit - 1), there


def spread_pivot(cols, front_index, front_count, holders):
    leaf_index = lax.axis_index("leaf")
    half = S // 2
    mine = lax.dynamic_slice_in_dim(cols, leaf_index * half, half, 0)
    steps = []
    step = holders
    while step < front_count:
        steps.append(step)
        step *= 2
    pieces = []
    for order, part in ((steps, mine[:half // 2]), (steps[::-1], mine[half // 2:])):
        held = list(range(holders))
        part = jnp.where(front_index < holders, part, 0.0)
        for step in order:
            got = lax.ppermute(part, "front", [(f, f + step) for f in held])
            part = part + got
            held += [f + step for f in held]
        pieces.append(part)
    mine = jnp.concatenate(pieces, axis=0)
    if holders > 1:
        groups = [list(range(f, f + holders)) for f in range(0, front_count, holders)]
        mine = lax.all_gather(mine, "front", axis_index_groups=groups, axis=1, tiled=True)
    other = lax.ppermute(mine, "leaf", [(0, 1), (1, 0)])
    low = jnp.where(leaf_index == 0, mine, other)
    high = jnp.where(leaf_index == 0, other, mine)
    return jnp.concatenate([low, high], axis=0)


def per_device(front_block, child_update, child_map):
    row_count, col_count = front_block.shape
    front_count = lax.axis_size("front")
    leaf_index = lax.axis_index("leaf")
    front_index = lax.axis_index("front")
    place = jnp.stack([front_index, leaf_index]).astype(jnp.int32)
    swap = [(0, 1), (1, 0)]
    child = child_update[0]
    blocks = child_map[0]
    child_blocks = blocks.shape[0]
    parent_blocks = row_count // BLK

    placed = []
    for b in range(S // BLK):
        total = jnp.where(leaf_index == 0, front_block[b * BLK:(b + 1) * BLK], 0.0)
        for k in range(b + 1):
            total = total + jnp.where(blocks[k] == b, child[k * BLK:(k + 1) * BLK], 0.0)
        placed.append(total)
    placed = jnp.concatenate(placed, axis=0)
    cols = placed + lax.ppermute(placed, "leaf", swap)

    half = front_count // 2
    piece = cols.T
    pairs = [(f, f + half) for f in range(half)]
    pairs += [(front_count + f + half, front_count + f) for f in range(half)]
    came = lax.ppermute(piece, ("leaf", "front"), pairs)
    piece = jnp.where((front_index >= half) == (leaf_index == 1), piece, came)
    groups = [list(range(half)), list(range(half, front_count))]
    panel = lax.all_gather(piece, "front", axis_index_groups=groups, axis=0, tiled=True)

    diag = spread_pivot(cols, front_index, front_count, S // col_count)

    sent = lax.dynamic_slice_in_dim(
        child, (1 - leaf_index) * (child_blocks - parent_blocks) * BLK, row_count, 0)
    recv = lax.ppermute(sent, "leaf", swap)
    other_blocks = lax.ppermute(blocks, "leaf", swap)
    first = leaf_index * parent_blocks
    shift = leaf_index * (child_blocks - parent_blocks)
    index = jnp.stack(
        block_places(blocks, first, parent_blocks, 0, child_blocks)
        + block_places(other_blocks, first, parent_blocks, shift, parent_blocks))
    base = assemble(index, front_block, child, recv)

    top, mult = factor_and_solve(place, diag, cols)
    return finish(place, base, panel, mult, top)


def solution(mesh):
    return jax.shard_map(
        per_device,
        mesh=mesh,
        in_specs=(P("leaf", "front"), P("leaf", None, "front"), P("leaf", None)),
        out_specs=P("leaf", "front"),
        check_vma=False,
    )
```

time: 608 us -> 265 us (0.44); the launches traced: 599 us -> 264 us
  waiting for transfers between devices: 290 us -> 121 us
  other arithmetic: 150 us -> 4.12 us
  Pallas kernels: 0 us -> 66.5 us
  matrix products: 57.9 us -> 0 us
  local copies, waits for them, and re-layouts: 73.8 us -> 22.4 us
  starting transfers between devices: 9.98 us -> 29.8 us
    psum x2 -> x0, waiting for transfers between devices: 277 us -> none  [the longest x1 257 us: per_device(): pivot_panel = lax.psum(placed, 'front')]
    another operation x17 -> x2, other arithmetic: 120 us -> 0.68 us  [the longest x1 0.6 us: per_device(): jnp.stack(block_places(blocks, first, parent_blocks, 0, child_blocks) + b...]
    ppermute x0 -> x13, waiting for transfers between devices: none -> 85.6 us  [the longest x8 70.1 us: spread_pivot(): got = lax.ppermute(part, 'front', [(f, f + step) for f in held])]
    pallas_call x0 -> x3, Pallas kernels: none -> 66.5 us  [the longest x1 34.7 us: factor_and_solve(): pl.pallas_call(factor_kernel, out_shape=[jax.ShapeDtypeStruct((S, cc), jn...]
    another operation x20 -> x0, matrix products: 36.6 us -> none  [the longest x14 34.3 us: solve_right(): lax.linalg.triangular_solve(factor, rows, left_side=False, lower=True, tr...]
    all_gather x0 -> x1, waiting for transfers between devices: none -> 35.1 us  [per_device(): lax.all_gather(piece, 'front', axis_index_groups=groups, axis=0, tiled=True)]
    scatter x1 -> x0, local copies, waits for them, and re-layouts: 33.9 us -> none  [per_device(): jnp.zeros((P_SIZE, col_count), jnp.float32).at[row_index]]
    ppermute x0 -> x13, starting transfers between devices: none -> 29.8 us  [the longest x8 12.8 us: spread_pivot(): got = lax.ppermute(part, 'front', [(f, f + step) for f in held])]
  transfers between devices with their start and end apart: 3 -> 14, of which waited for: 3 -> 9; matrix products, arithmetic and copies ran while one was open for 0% -> 5% of each run, Pallas kernels for 0% -> 22%
where the time goes in v1:
time: 265 us; the launch traced here: 264 us
  waiting for transfers between devices  121 us (46%)
  Pallas kernels  66.5 us (25%)
  starting transfers between devices  29.8 us (11%)
  local copies, waits for them, and re-layouts  22.4 us (8%)
  between operations  20 us (8%)
  other arithmetic  4.12 us (2%)
    ppermute x8, waiting for transfers between devices, spread_pivot(): got = lax.ppermute(part, 'front', [(f, f + step) for f in held])  70.1 us
    all_gather x1, waiting for transfers between devices, per_device(): lax.all_gather(piece, 'front', axis_index_groups=groups, axis=0, tiled=True)  35.1 us
    pallas_call x1, Pallas kernels, factor_and_solve(): pl.pallas_call(factor_kernel, out_shape=[jax.ShapeDtypeStruct((S, cc), jn...  34.7 us
    pallas_call x1, Pallas kernels, assemble(): pl.pallas_call(assemble_kernel, out_shape=jax.ShapeDtypeStruct((rows, cc)...  22.8 us
    ppermute x8, starting transfers between devices, spread_pivot(): got = lax.ppermute(part, 'front', [(f, f + step) for f in held])  12.8 us
    ppermute x1, waiting for transfers between devices, per_device(): came = lax.ppermute(piece, ('leaf', 'front'), pairs)  12.3 us
    ppermute x1, starting transfers between devices, per_device(): recv = lax.ppermute(sent, 'leaf', swap)  10.3 us
    pallas_call x1, Pallas kernels, finish(): pl.pallas_call(finish_kernel, out_shape=jax.ShapeDtypeStruct((rows, cc),...  9.04 us
  transfers between devices with their start and end apart: 14, of which 9 were waited for; matrix products, arithmetic and copies ran while one was open for 5% of the time, Pallas kernels for 22%

profile of v1, /device:TPU:0, one launch (start us, length us, event | category | flops | bytes accessed | tf_op | source)
XLA Modules:
  0.0 263.6 jit_solution(16752223745643215370)
XLA Ops:
  6.5 1.5 fusion.3
  18.7 2.3 collective-permute-done.2
  21.2 5.9 %collective-permute-start.3 = (f32[512,512]{1,0:T(8,128)S(1)}, f32[512,512]{1,0:T(8,128)S(1)}, u32[]{:S(2)}, u32[]{:S(2)}) collective-permute-start(f32[512,512]{1,0:T(8,128)S(1)} %bitcast.57), channel_id=1, source_target_pairs={{0,8},{1,9},{2,10},{3,11},{4,12},{5,13},{6,14},{7,15},{24,16},{25,... | collective-permute-start | bytes 3145736 | tf_op jit(solution)/shard_map/ppermute | solution.py:277
  27.1 12.3 %collective-permute-done.3 = f32[512,512]{1,0:T(8,128)S(1)} collective-permute-done((f32[512,512]{1,0:T(8,128)S(1)}, f32[512,512]{1,0:T(8,128)S(1)}, u32[]{:S(2)}, u32[]{:S(2)}) %collective-permute-start.3) | collective-permute-done | bytes 1048608 | tf_op jit(solution)/shard_map/ppermute | solution.py:277
  40.6 7.8 %dynamic-slice_bitcast_fusion = f32[4096,512]{1,0:T(8,128)} fusion(f32[1,6144,512]{2,1,0:T(8,128)} %param.4, s32[]{:T(128)S(6)} %select_n.146), kind=kLoop, calls=%fused_computation | loop fusion | bytes 16777220 | tf_op jit(solution)/shard_map/dynamic_slice | solution.py:284
  48.4 10.3 %collective-permute-start.1 = (f32[4096,512]{1,0:T(8,128)}, f32[4096,512]{1,0:T(8,128)}, u32[]{:S(2)}, u32[]{:S(2)}) collective-permute-start(f32[4096,512]{1,0:T(8,128)} %dynamic-slice_bitcast_fusion), channel_id=1, source_target_pairs={{0,16},{16,0},{1,17},{17,1},{2,18},{18,2},{3,19},{19,3},{4,20},{20... | collective-permute-start | bytes 25165832 | tf_op jit(solution)/shard_map/ppermute | solution.py:286
  58.7 1.8 collective-permute-start.8
  60.5 3.0 %collective-permute-start.4 = (f32[128,512]{0,1:T(8,128)S(1)}, f32[128,512]{0,1:T(8,128)S(1)}, u32[]{:S(2)}, u32[]{:S(2)}) collective-permute-start(f32[128,512]{0,1:T(8,128)S(1)} %get-tuple-element.25), channel_id=1, source_target_pairs={{0,1},{16,17}} | collective-permute-start | bytes 786440 | tf_op jit(solution)/shard_map/ppermute | solution.py:238
  63.5 8.8 %collective-permute-done.8 = f32[128,512]{0,1:T(8,128)S(1)} collective-permute-done((f32[128,512]{0,1:T(8,128)S(1)}, f32[128,512]{0,1:T(8,128)S(1)}, u32[]{:S(2)}, u32[]{:S(2)}) %collective-permute-start.8) | collective-permute-done | bytes 262176 | tf_op jit(solution)/shard_map/ppermute | solution.py:238
  72.4 1.3 collective-permute-start.9
  73.7 23.7 %collective-permute-done.4 = f32[128,512]{0,1:T(8,128)S(1)} collective-permute-done((f32[128,512]{0,1:T(8,128)S(1)}, f32[128,512]{0,1:T(8,128)S(1)}, u32[]{:S(2)}, u32[]{:S(2)}) %collective-permute-start.4) | collective-permute-done | bytes 262176 | tf_op jit(solution)/shard_map/ppermute | solution.py:238
  97.4 1.3 collective-permute-start.5
  98.7 1.3 collective-permute-start.10
  100.1 8.8 %collective-permute-done.5 = f32[128,512]{0,1:T(8,128)S(1)} collective-permute-done((f32[128,512]{0,1:T(8,128)S(1)}, f32[128,512]{0,1:T(8,128)S(1)}, u32[]{:S(2)}, u32[]{:S(2)}) %collective-permute-start.5) | collective-permute-done | bytes 262176 | tf_op jit(solution)/shard_map/ppermute | solution.py:238
  110.3 9.8 %collective-permute-done.10 = f32[128,512]{0,1:T(8,128)S(1)} collective-permute-done((f32[128,512]{0,1:T(8,128)S(1)}, f32[128,512]{0,1:T(8,128)S(1)}, u32[]{:S(2)}, u32[]{:S(2)}) %collective-permute-start.10) | collective-permute-done | bytes 262176 | tf_op jit(solution)/shard_map/ppermute | solution.py:238
  121.5 1.5 collective-permute-start.7
  123.3 19.0 %collective-permute-done.11 = f32[128,512]{0,1:T(8,128)S(1)} collective-permute-done((f32[128,512]{0,1:T(8,128)S(1)}, f32[128,512]{0,1:T(8,128)S(1)}, u32[]{:S(2)}, u32[]{:S(2)}) %collective-permute-start.11) | collective-permute-done | bytes 262176 | tf_op jit(solution)/shard_map/ppermute | solution.py:238
  145.8 1.3 copy.22.diag_ref
  148.3 34.7 %factor_and_solve.1 = (f32[512,512]{1,0:T(8,128)S(1)}, f32[512,512]{1,0:T(8,128)S(1)}) custom-call(s32[2]{0:T(128)S(1)} %pad_add_fusion.1.place, f32[512,512]{1,0:T(8,128)S(1)} %copy-done.2, f32[512,512]{1,0:T(8,128)S(1)} %copy.23.cols_ref), custom_call_target="tpu_custom_call" | custom-call | flops 4831838208 | bytes 4194304 | tf_op jit(solution)/shard_map/factor_and_solve/pallas_call | solution.py:131
  183.1 22.8 %assemble.1.base_ref = f32[4096,512]{1,0:T(8,128)} custom-call(s32[4,32]{1,0:T(4,128)} %pad_add_fusion.index, f32[4096,512]{1,0:T(8,128)} %front_ref.1, f32[6144,512]{1,0:T(8,128)} %bitcast.56, f32[4096,512]{1,0:T(8,128)} %collective-permute-done.1.recv_ref), custom_call_target="tpu_custom_call" | custom-call | flops 4194304 | bytes 33554432 | tf_op jit(solution)/shard_map/assemble/pallas_call | solution.py:154
  205.8 35.1 %all-gather.2.cloned.1.call-done.panel_ref = f32[4096,512]{1,0:T(8,128)} async-done(((f32[512,512]{1,0:T(8,128)}), f32[4096,512]{1,0:T(8,128)}) %all-gather.2.cloned.1.call-update) | async-done | bytes 8388624 | tf_op jit(solution)/shard_map/all_gather | solution.py:280
  241.0 3.4 %copy-done = f32[4096,512]{1,0:T(8,128)S(1)} copy-done((f32[4096,512]{1,0:T(8,128)S(1)}, f32[4096,512]{1,0:T(8,128)}, u32[]{:S(2)}) %copy-start) | copy-done | bytes 8388632
  244.3 3.4 %copy-done.1 = f32[4096,512]{1,0:T(8,128)S(1)} copy-done((f32[4096,512]{1,0:T(8,128)S(1)}, f32[4096,512]{1,0:T(8,128)}, u32[]{:S(2)}) %copy-start.1) | copy-done | bytes 8388632
  247.7 9.0 %finish.1 = f32[4096,512]{1,0:T(8,128)} custom-call(s32[2]{0:T(128)S(1)} %pad_add_fusion.1.place, f32[4096,512]{1,0:T(8,128)S(1)} %copy-done, f32[4096,512]{1,0:T(8,128)S(1)} %copy-done.1, f32[512,512]{1,0:T(8,128)S(1)} %get-tuple-element.7.mult_ref, f32[512,512]{1,0:T(8,128)S(1)} %get-tuple-element.8.top_ref), custom_call_target="tpu_custom_call" | custom-call | flops 6442450944 | bytes 25165824 | tf_op jit(solution)/shard_map/finish/pallas_call | solution.py:195
  (52 shorter events, 13.6 us)
Async XLA Ops:
  6.5 234.4 %all-gather.2.cloned.1.call-start = ((), (), s32[]{:S(2)}) async-start(), calls=%async_computation | async-start | bytes 9437184 | tf_op jit(solution)/shard_map/all_gather | solution.py:280
  18.2 2.8 %collective-permute-start.2 = (f32[512,512]{0,1:T(8,128)S(1)}, f32[512,512]{0,1:T(8,128)S(1)}, u32[]{:S(2)}, u32[]{:S(2)}) collective-permute-start(f32[512,512]{0,1:T(8,128)S(1)} %pad_maximum_fusion), channel_id=1, source_target_pairs={{0,16},{16,0},{1,17},{17,1},{2,18},{18,2},{3,19},{19,3},{4,20},{20... | collective-permute-start | bytes 3145736 | tf_op jit(solution)/shard_map/ppermute | solution.py:271
  21.2 18.2 %collective-permute-start.3 = (f32[512,512]{1,0:T(8,128)S(1)}, f32[512,512]{1,0:T(8,128)S(1)}, u32[]{:S(2)}, u32[]{:S(2)}) collective-permute-start(f32[512,512]{1,0:T(8,128)S(1)} %bitcast.57), channel_id=1, source_target_pairs={{0,8},{1,9},{2,10},{3,11},{4,12},{5,13},{6,14},{7,15},{24,16},{25,... | collective-permute-start | bytes 3145736 | tf_op jit(solution)/shard_map/ppermute | solution.py:277
  40.6 69.6 %copy-start.3 = (s32[1,48]{1,0:T(1,128)S(1)}, s32[1,48]{1,0:T(1,128)}, u32[]{:S(2)}) copy-start(s32[1,48]{1,0:T(1,128)} %param.5) | copy-start | bytes 580
  48.4 134.7 %collective-permute-start.1 = (f32[4096,512]{1,0:T(8,128)}, f32[4096,512]{1,0:T(8,128)}, u32[]{:S(2)}, u32[]{:S(2)}) collective-permute-start(f32[4096,512]{1,0:T(8,128)} %dynamic-slice_bitcast_fusion), channel_id=1, source_target_pairs={{0,16},{16,0},{1,17},{17,1},{2,18},{18,2},{3,19},{19,3},{4,20},{20... | collective-permute-start | bytes 25165832 | tf_op jit(solution)/shard_map/ppermute | solution.py:286
  58.7 13.6 %collective-permute-start.8 = (f32[128,512]{0,1:T(8,128)S(1)}, f32[128,512]{0,1:T(8,128)S(1)}, u32[]{:S(2)}, u32[]{:S(2)}) collective-permute-start(f32[128,512]{0,1:T(8,128)S(1)} %get-tuple-element.26), channel_id=1, source_target_pairs={{0,8},{16,24}} | collective-permute-start | bytes 786440 | tf_op jit(solution)/shard_map/ppermute | solution.py:238
  60.5 36.8 %collective-permute-start.4 = (f32[128,512]{0,1:T(8,128)S(1)}, f32[128,512]{0,1:T(8,128)S(1)}, u32[]{:S(2)}, u32[]{:S(2)}) collective-permute-start(f32[128,512]{0,1:T(8,128)S(1)} %get-tuple-element.25), channel_id=1, source_target_pairs={{0,1},{16,17}} | collective-permute-start | bytes 786440 | tf_op jit(solution)/shard_map/ppermute | solution.py:238
  72.4 26.3 %collective-permute-start.9 = (f32[128,512]{0,1:T(8,128)S(1)}, f32[128,512]{0,1:T(8,128)S(1)}, u32[]{:S(2)}, u32[]{:S(2)}) collective-permute-start(f32[128,512]{0,1:T(8,128)S(1)} %add.112), channel_id=1, source_target_pairs={{0,4},{8,12},{16,20},{24,28}} | collective-permute-start | bytes 786440 | tf_op jit(solution)/shard_map/ppermute | solution.py:238
  97.4 11.5 %collective-permute-start.5 = (f32[128,512]{0,1:T(8,128)S(1)}, f32[128,512]{0,1:T(8,128)S(1)}, u32[]{:S(2)}, u32[]{:S(2)}) collective-permute-start(f32[128,512]{0,1:T(8,128)S(1)} %add.108), channel_id=1, source_target_pairs={{0,2},{1,3},{16,18},{17,19}} | collective-permute-start | bytes 786440 | tf_op jit(solution)/shard_map/ppermute | solution.py:238
  98.7 21.4 %collective-permute-start.10 = (f32[128,512]{0,1:T(8,128)S(1)}, f32[128,512]{0,1:T(8,128)S(1)}, u32[]{:S(2)}, u32[]{:S(2)}) collective-permute-start(f32[128,512]{0,1:T(8,128)S(1)} %add.113), channel_id=1, source_target_pairs={{0,2},{8,10},{4,6},{12,14},{16,18},{24,26},{20,22},{28,30}} | collective-permute-start | bytes 786440 | tf_op jit(solution)/shard_map/ppermute | solution.py:238
  108.9 12.5 %collective-permute-start.6 = (f32[128,512]{0,1:T(8,128)S(1)}, f32[128,512]{0,1:T(8,128)S(1)}, u32[]{:S(2)}, u32[]{:S(2)}) collective-permute-start(f32[128,512]{0,1:T(8,128)S(1)} %add.109), channel_id=1, source_target_pairs={{0,4},{1,5},{2,6},{3,7},{16,20},{17,21},{18,22},{19,23}} | collective-permute-start | bytes 786440 | tf_op jit(solution)/shard_map/ppermute | solution.py:238
  110.2 12.8 %collective-permute-start = (s32[48]{0:T(128)S(1)}, s32[48]{0:T(128)S(1)}, u32[]{:S(2)}, u32[]{:S(2)}) collective-permute-start(s32[48]{0:T(128)S(1)} %bitcast.58), channel_id=1, source_target_pairs={{0,16},{16,0},{1,17},{17,1},{2,18},{18,2},{3,19},{19,3},{4,20},{20... | collective-permute-start | bytes 584 | tf_op jit(solution)/shard_map/ppermute | solution.py:287
  120.1 22.1 %collective-permute-start.11 = (f32[128,512]{0,1:T(8,128)S(1)}, f32[128,512]{0,1:T(8,128)S(1)}, u32[]{:S(2)}, u32[]{:S(2)}) collective-permute-start(f32[128,512]{0,1:T(8,128)S(1)} %add.114), channel_id=1, source_target_pairs={{0,1},{8,9},{4,5},{12,13},{2,3},{10,11},{6,7},{14,15},{16,17},{24,... | collective-permute-start | bytes 786440 | tf_op jit(solution)/shard_map/ppermute | solution.py:238
  121.5 20.8 %collective-permute-start.7 = (f32[128,512]{0,1:T(8,128)S(1)}, f32[128,512]{0,1:T(8,128)S(1)}, u32[]{:S(2)}, u32[]{:S(2)}) collective-permute-start(f32[128,512]{0,1:T(8,128)S(1)} %add.110), channel_id=1, source_target_pairs={{0,8},{1,9},{2,10},{3,11},{4,12},{5,13},{6,14},{7,15},{16,24},{17,... | collective-permute-start | bytes 786440 | tf_op jit(solution)/shard_map/ppermute | solution.py:238
  142.4 2.1 collective-permute-start.12
  147.1 1.2 copy-start.2
  241.0 3.4 %copy-start = (f32[4096,512]{1,0:T(8,128)S(1)}, f32[4096,512]{1,0:T(8,128)}, u32[]{:S(2)}) copy-start(f32[4096,512]{1,0:T(8,128)} %assemble.1.base_ref) | copy-start | bytes 25165828
  244.3 3.4 %copy-start.1 = (f32[4096,512]{1,0:T(8,128)S(1)}, f32[4096,512]{1,0:T(8,128)}, u32[]{:S(2)}) copy-start(f32[4096,512]{1,0:T(8,128)} %all-gather.2.cloned.1.call-done.panel_ref) | copy-start | bytes 25165828
Sparse Core Ops, SparseCore 0:
  40.7 200.2 all-gather.1
